TPU v7x, 128 devices: a whole 4x4x4 slice. The times are simulated.
128 devices in a mesh: section: 2 (over x_lo), dp: 8 (over x_hi, y), tensor: 8 (over z, core).
Axes of the slice: x: 4 (x_hi: 2, x_lo: 2; x = x_hi * 2 + x_lo), y: 4, z: 4, core: 2. Of those that a mesh axis runs over, the one named last changes fastest.
Arguments:
- tokens: bfloat16 [2048, 8192], P('dp', ('section', 'tensor')), may hold values from -6 to 6
- segment_ids: int32 [8, 256], P('dp'), may hold values from 0 to 3, never falling along the last dimension, each value on 1 to 128 neighbouring positions
- gain_attn: float32 [8192], replicated, may hold values from 0.1 to 1.9
- w_query: bfloat16 [8192, 4096], P(None, ('section', 'tensor')), may hold values from -0.06629126 to 0.06629126
- w_key: bfloat16 [8192, 4096], P(None, ('section', 'tensor')), may hold values from -0.06629126 to 0.06629126
- w_value: bfloat16 [8192, 4096], P(None, ('section', 'tensor')), may hold values from -0.0625 to 0.0625
- w_output: bfloat16 [4096, 8192], P(('section', 'tensor')), may hold values from -0.09375 to 0.09375
- gain_ffn: float32 [8192], replicated, may hold values from 0.1 to 1.9
- w_up: bfloat16 [8192, 16384], P(('section', 'tensor'), 'dp'), may hold values from -0.0625 to 0.0625
- w_down: bfloat16 [16384, 8192], P('dp', ('section', 'tensor')), may hold values from -0.046875 to 0.046875
Outputs:
- layer_out: bfloat16 [2048, 8192], P('dp', ('section', 'tensor'))
Inputs may be any that keep to these rules, and one draw needn't show every extreme that they name: `segment_ids`: segment numbers never fall along a replica's tokens; each segment holds 1 to 128 tokens.
All inputs are finite; a program needn't handle non-finite values.
Results may differ from a plain program's by a relative error of at most 0.023.
Values may be sent and summed in bfloat16 or wider, within the bound.
A program may use at most 128 MiB of HBM per device.

v0:
```python
import jax
import jax.numpy as jnp
from jax import lax
from jax.sharding import PartitionSpec as P

HD = 128


def layer_norm(values, gain):
    mean = jnp.mean(values, axis=-1, keepdims=True)
    second = jnp.mean(values * values, axis=-1, keepdims=True)
    return (values - mean) * lax.rsqrt(second - mean * mean + 1e-05) * gain


def per_device(
    tokens, segment_ids, gain_attn, w_query, w_key, w_value, w_output, gain_ffn, w_up, w_down
):
    tok_rows = tokens.shape[0]
    width = gain_attn.shape[0]
    groups = lax.axis_size(("section", "tensor"))
    share = width // groups
    first_col = lax.axis_index(("section", "tensor")) * share
    whole = lax.all_gather(tokens, ("section", "tensor"), axis=1, tiled=True)
    normed = layer_norm(whole.astype(jnp.float32), gain_attn).astype(jnp.bfloat16)
    local_heads = w_query.shape[1] // HD
    query = jnp.dot(normed, w_query, preferred_element_type=jnp.float32).astype(jnp.bfloat16)
    key = jnp.dot(normed, w_key, preferred_element_type=jnp.float32).astype(jnp.bfloat16)
    value = jnp.dot(normed, w_value, preferred_element_type=jnp.float32).astype(jnp.bfloat16)
    query = query.reshape(tok_rows, local_heads, HD)
    key = key.reshape(tok_rows, local_heads, HD)
    value = value.reshape(tok_rows, local_heads, HD)
    scores = jnp.einsum("qhd,khd->hqk", query, key, preferred_element_type=jnp.float32) * HD ** (
        -0.5
    )
    position = jnp.arange(tok_rows)
    segment_row = segment_ids[0]
    keep = jnp.logical_and(
        position[:, None] >= position[None, :], segment_row[:, None] == segment_row[None, :]
    )
    scores = jnp.where(keep[None], scores, -1e30)
    top = jnp.max(scores, axis=-1, keepdims=True)
    expo = jnp.exp(scores - top)
    probs = (expo / jnp.sum(expo, axis=-1, keepdims=True)).astype(jnp.bfloat16)
    context = jnp.einsum("hqk,khd->qhd", probs, value, preferred_element_type=jnp.float32)
    context = context.astype(jnp.bfloat16).reshape(tok_rows, local_heads * HD)
    partial_out = jnp.dot(context, w_output, preferred_element_type=jnp.float32)
    summed = lax.psum(partial_out.astype(jnp.bfloat16), ("section", "tensor")).astype(jnp.float32)
    resid_full = (whole.astype(jnp.float32) + summed).astype(jnp.bfloat16)
    normed_full = layer_norm(resid_full.astype(jnp.float32), gain_ffn).astype(jnp.bfloat16)
    normed_ffn = lax.dynamic_slice_in_dim(normed_full, first_col, share, 1)
    resid_mid = lax.dynamic_slice_in_dim(resid_full, first_col, share, 1)
    gathered = lax.all_gather(normed_ffn, "dp", axis=0, tiled=True)
    pre_act = lax.psum_scatter(
        jnp.dot(gathered, w_up, preferred_element_type=jnp.float32).astype(jnp.bfloat16),
        ("section", "tensor"),
        scatter_dimension=0,
        tiled=True,
    ).astype(jnp.float32)
    activated = jax.nn.gelu(pre_act, approximate=True).astype(jnp.bfloat16)
    partial_down = jnp.dot(
        lax.all_gather(activated, ("section", "tensor"), axis=0, tiled=True),
        w_down,
        preferred_element_type=jnp.float32,
    )
    ffn_out = lax.psum_scatter(
        partial_down.astype(jnp.bfloat16), "dp", scatter_dimension=0, tiled=True
    ).astype(jnp.float32)
    return (resid_mid.astype(jnp.float32) + ffn_out).astype(jnp.bfloat16)


def solution(mesh):
    return jax.shard_map(
        per_device,
        mesh=mesh,
        in_specs=(
            P("dp", ("section", "tensor")),
            P("dp", None),
            P(),
            P(None, ("section", "tensor")),
            P(None, ("section", "tensor")),
            P(None, ("section", "tensor")),
            P(("section", "tensor"), None),
            P(),
            P(("section", "tensor"), "dp"),
            P("dp", ("section", "tensor")),
        ),
        out_specs=P("dp", ("section", "tensor")),
        check_vma=False,
    )
```

profile of v0, /device:TPU:0, one launch (start us, length us, event | category | flops | bytes accessed | tf_op | source)
XLA Modules:
  0.0 492.6 jit_solution(8370720796275052697)
XLA Ops:
  6.5 0.0 copy-start
  6.5 0.0 copy-start.7
  6.5 0.0 all-gather.4.cloned.1.call-start
  6.5 0.7 all-gather.4.cloned.1.call-update
  7.3 0.0 all-reduce.2.cloned.1.call-start
  7.3 0.9 fusion.18
  8.2 40.8 %all-gather.4.cloned.1.call-done = bf16[256,8192]{1,0:T(8,128)(2,1)} async-done(((bf16[256,512]{1,0:T(8,128)(2,1)}), bf16[256,8192]{1,0:T(8,128)(2,1)}) %all-gather.4.cloned.1.call-update) | async-done | bytes 4194320 | tf_op jit(solution)/shard_map/all_gather | solution.py:23
  49.0 3.5 convert_reduce_fusion
  52.5 0.0 copy-done.7
  52.5 0.0 copy-done.3
  52.5 0.0 copy-start.5
  52.5 1.8 fusion.3
  54.3 0.4 copy-done.5
  54.7 1.8 convolution_convert_fusion.4
  56.6 0.3 copy-done.2
  56.9 1.6 copy-done.6
  58.4 1.8 convolution_convert_fusion.5
  60.3 0.4 fusion.23
  60.7 0.3 fusion.8
  60.9 5.2 %convolution_convert_fusion.6 = bf16[256,256]{0,1:T(8,128)(2,1)S(1)} fusion(bf16[256,8192]{1,0:T(8,128)(2,1)} %copy-done.2, bf16[8192,256]{1,0:T(8,128)(2,1)} %param.15), kind=kOutput, calls=%fused_computation.26 | convolution fusion | flops 1073807360 | bytes 8519680 | tf_op jit(solution)/shard_map/dot_general | solution.py:28
  66.1 0.3 convolution_convert_fusion.3
  66.4 5.4 %convolution_convert_fusion = bf16[256,8192]{1,0:T(8,128)(2,1)} fusion(bf16[256,256]{0,1:T(8,128)(2,1)S(1)} %bitcast.30, bf16[256,8192]{1,0:T(8,128)(2,1)} %param.16), kind=kOutput, calls=%fused_computation.5 | convolution fusion | flops 1075838976 | bytes 8519680 | tf_op jit(solution)/shard_map/dot_general | solution.py:46
  71.9 0.0 all-reduce.2.cloned.1.call-update
  71.9 0.2 all-gather.6.cloned.1.call-start
  72.1 0.8 dynamic-slice
  72.9 128.7 %all-reduce.2.cloned.1.call-done = bf16[256,8192]{1,0:T(8,128)(2,1)} async-done(((bf16[256,8192]{1,0:T(8,128)(2,1)}), bf16[256,8192]{1,0:T(8,128)(2,1)}) %all-reduce.2.cloned.1.call-update) | async-done | bytes 4194320 | tf_op jit(solution)/shard_map/psum | solution.py:47
  201.6 4.6 convert_reduce_fusion.1
  206.2 0.0 copy-start.4
  206.2 1.0 convert_element_type.73
  207.2 1.0 copy-done.4
  208.2 0.9 fusion.17
  209.0 0.0 all-gather.6.cloned.1.call-update
  209.1 0.0 reduce-scatter.3.cloned.1.call-start
  209.1 54.6 %all-gather.6.cloned.1.call-done = bf16[2048,512]{1,0:T(8,128)(2,1)} async-done(((bf16[256,512]{1,0:T(8,128)(2,1)}), bf16[2048,512]{1,0:T(8,128)(2,1)}) %all-gather.6.cloned.1.call-update) | async-done | bytes 2097168 | tf_op jit(solution)/shard_map/all_gather | solution.py:52
  263.7 0.0 copy-done
  263.7 8.3 %convolution_convert_fusion.1 = bf16[2048,2048]{1,0:T(8,128)(2,1)} fusion(bf16[2048,512]{1,0:T(8,128)(2,1)} %all-gather.6.cloned.1.call-done, bf16[512,2048]{1,0:T(8,128)(2,1)S(1)} %copy-done), kind=kOutput, calls=%fused_computation.12 | convolution fusion | flops 4299161600 | bytes 12582912 | tf_op jit(solution)/shard_map/dot_general | solution.py:54
  272.0 0.0 reduce-scatter.3.cloned.1.call-update
  272.0 0.0 all-gather.8.cloned.1.call-start
  272.1 73.0 %reduce-scatter.3.cloned.1.call-done = bf16[128,2048]{1,0:T(8,128)(2,1)} async-done(((bf16[2048,2048]{1,0:T(8,128)(2,1)}), bf16[128,2048]{1,0:T(8,128)(2,1)}) %reduce-scatter.3.cloned.1.call-update) | async-done | bytes 524304 | tf_op jit(solution)/shard_map/reduce_scatter | solution.py:53
  345.1 2.2 fusion.14
  347.4 0.0 all-gather.8.cloned.1.call-update
  347.4 0.0 reduce-scatter.5.cloned.1.call-start
  347.5 50.4 %all-gather.8.cloned.1.call-done = bf16[2048,2048]{1,0:T(8,128)(2,1)} async-done(((bf16[128,2048]{1,0:T(8,128)(2,1)}), bf16[2048,2048]{1,0:T(8,128)(2,1)}) %all-gather.8.cloned.1.call-update) | async-done | bytes 8388624 | tf_op jit(solution)/shard_map/all_gather | solution.py:61
  397.9 10.0 %convolution_convert_fusion.2 = bf16[2048,512]{1,0:T(8,128)(2,1)} fusion(bf16[2048,2048]{1,0:T(8,128)(2,1)} %all-gather.8.cloned.1.call-done, bf16[2048,512]{1,0:T(8,128)(2,1)} %param.19), kind=kOutput, calls=%fused_computation.14 | convolution fusion | flops 4296015872 | bytes 12582912 | tf_op jit(solution)/shard_map/dot_general | solution.py:60
  407.9 0.0 reduce-scatter.5.cloned.1.call-update
  407.9 76.0 %reduce-scatter.5.cloned.1.call-done = bf16[256,512]{1,0:T(8,128)(2,1)} async-done(((bf16[2048,512]{1,0:T(8,128)(2,1)}), bf16[256,512]{1,0:T(8,128)(2,1)}) %reduce-scatter.5.cloned.1.call-update) | async-done | bytes 262160 | tf_op jit(solution)/shard_map/reduce_scatter | solution.py:65
  484.0 1.8 add_convert_fusion
  485.8 0.0 copy-done.1
  (6 shorter events, 0.0 us)
Async XLA Ops:
  6.5 257.2 %copy-start = (bf16[512,2048]{1,0:T(8,128)(2,1)S(1)}, bf16[512,2048]{1,0:T(8,128)(2,1)}, u32[]{:S(2)}) copy-start(bf16[512,2048]{1,0:T(8,128)(2,1)} %param.18) | copy-start | bytes 6291460
  6.5 46.0 %copy-start.7 = (f32[8192]{0:T(1024)S(1)}, f32[8192]{0:T(1024)}, u32[]{:S(2)}) copy-start(f32[8192]{0:T(1024)} %param.12) | copy-start | bytes 98308
  6.5 42.4 %all-gather.4.cloned.1.call-start = ((), (), s32[]{:S(2)}) async-start(), calls=%async_computation.2 | async-start | bytes 4456448 | tf_op jit(solution)/shard_map/all_gather | solution.py:23
  7.3 194.3 %all-reduce.2.cloned.1.call-start = ((), (), s32[]{:S(2)}) async-start(), calls=%async_computation.3 | async-start | bytes 8388608 | tf_op jit(solution)/shard_map/psum | solution.py:47
  49.0 3.6 copy-start.3
  52.5 2.2 copy-start.5
  54.7 2.1 copy-start.2
  54.7 3.7 copy-start.6
  71.9 191.8 %all-gather.6.cloned.1.call-start = ((), (), s32[]{:S(2)}) async-start(), calls=%async_computation.4 | async-start | bytes 2359296 | tf_op jit(solution)/shard_map/all_gather | solution.py:52
  206.2 2.0 copy-start.4
  209.1 136.1 %reduce-scatter.3.cloned.1.call-start = ((), (), s32[]{:S(2)}) async-start(), calls=%async_computation.5 | async-start | bytes 8912896 | tf_op jit(solution)/shard_map/reduce_scatter | solution.py:53
  272.0 125.8 %all-gather.8.cloned.1.call-start = ((), (), s32[]{:S(2)}) async-start(), calls=%async_computation.6 | async-start | bytes 8912896 | tf_op jit(solution)/shard_map/all_gather | solution.py:61
  347.4 136.6 %reduce-scatter.5.cloned.1.call-start = ((), (), s32[]{:S(2)}) async-start(), calls=%async_computation.7 | async-start | bytes 2359296 | tf_op jit(solution)/shard_map/reduce_scatter | solution.py:65
  397.9 87.9 %copy-start.1 = (bf16[512,2048]{1,0:T(8,128)(2,1)S(1)}, bf16[512,2048]{1,0:T(8,128)(2,1)}, u32[]{:S(2)}) copy-start(bf16[512,2048]{1,0:T(8,128)(2,1)} %param.18) | copy-start | bytes 6291460
Sparse Core Ops, SparseCore 0:
  9.0 39.8 all-gather.3
  72.0 129.5 all-reduce.1
  209.2 54.4 all-gather.5
  272.2 72.9 reduce-scatter.2
  347.5 50.3 all-gather.7
  408.0 75.8 reduce-scatter.4
where the time goes:
time: 493 us
  waiting for transfers between devices  424 us (86%)
  matrix products  33.5 us (7%)
  other arithmetic  16.6 us (3%)
  between operations  13.6 us (3%)
    psum x1, waiting for transfers between devices, per_device(): lax.psum(partial_out.astype(jnp.bfloat16), ('section', 'tensor'))  129 us
    reduce_scatter x1, waiting for transfers between devices, per_device(): lax.psum_scatter(partial_down.astype(jnp.bfloat16), 'dp', scatter_dimensi...  76 us
    reduce_scatter x1, waiting for transfers between devices, per_device(): lax.psum_scatter(jnp.dot(gathered, w_up, preferred_element_type=jnp.float...  73 us
    all_gather x1, waiting for transfers between devices, per_device(): gathered = lax.all_gather(normed_ffn, 'dp', axis=0, tiled=True)  54.6 us
    all_gather x1, waiting for transfers between devices, per_device(): lax.all_gather(activated, ('section', 'tensor'), axis=0, tiled=True)  50.4 us
    all_gather x1, waiting for transfers between devices, per_device(): whole = lax.all_gather(tokens, ('section', 'tensor'), axis=1, tiled=True)  40.8 us
    dot_general x1, matrix products, per_device(): jnp.dot(lax.all_gather(activated, ('section', 'tensor'), axis=0, tiled=Tr...  9.99 us
  transfers between devices with their start and end apart: 6, of which 6 were waited for; matrix products, arithmetic and copies ran while one was open for 0% of the time, Pallas kernels for 0%

commit v1 on v0

--- a/solution.py
+++ b/solution.py
@@ -2,6 +2,7 @@
 import jax.numpy as jnp
 from jax import lax
 from jax.sharding import PartitionSpec as P
+from jax.lax import psum
 
 HD = 128
 
@@ -15,6 +16,12 @@
 def per_device(
     tokens, segment_ids, gain_attn, w_query, w_key, w_value, w_output, gain_ffn, w_up, w_down
 ):
+
+    def advance_classes_up(base_x, axis_name, peer_axis):
+        for src_i in (axis_name, peer_axis):
+            base_x = psum(base_x, src_i)
+        return base_x
+
     tok_rows = tokens.shape[0]
     width = gain_attn.shape[0]
     groups = lax.axis_size(("section", "tensor"))
@@ -44,7 +51,9 @@
     context = jnp.einsum("hqk,khd->qhd", probs, value, preferred_element_type=jnp.float32)
     context = context.astype(jnp.bfloat16).reshape(tok_rows, local_heads * HD)
     partial_out = jnp.dot(context, w_output, preferred_element_type=jnp.float32)
-    summed = lax.psum(partial_out.astype(jnp.bfloat16), ("section", "tensor")).astype(jnp.float32)
+    summed = advance_classes_up(partial_out.astype(jnp.bfloat16), "section", "tensor").astype(
+        jnp.float32
+    )
     resid_full = (whole.astype(jnp.float32) + summed).astype(jnp.bfloat16)
     normed_full = layer_norm(resid_full.astype(jnp.float32), gain_ffn).astype(jnp.bfloat16)
     normed_ffn = lax.dynamic_slice_in_dim(normed_full, first_col, share, 1)

time: 493 us -> 554 us (1.12)
  waiting for transfers between devices: 424 us -> 485 us
    psum x1 -> x2, waiting for transfers between devices: 129 us -> 190 us  [advance_classes_up(): base_x = psum(base_x, src_i)]
  transfers between devices with their start and end apart: 6 -> 7, of which waited for: 6 -> 7; matrix products, arithmetic and copies ran while one was open for 0% -> 0% of each run, Pallas kernels for 0% -> 0%
where the time goes in v1:
time: 554 us; the launch traced here: 553 us
  waiting for transfers between devices  485 us (88%)
  matrix products  33.5 us (6%)
  other arithmetic  16.6 us (3%)
  between operations  13.6 us (2%)
    psum x2, waiting for transfers between devices, advance_classes_up(): base_x = psum(base_x, src_i)  190 us
    reduce_scatter x1, waiting for transfers between devices, per_device(): lax.psum_scatter(partial_down.astype(jnp.bfloat16), 'dp', scatter_dimensi...  76.1 us
    reduce_scatter x1, waiting for transfers between devices, per_device(): lax.psum_scatter(jnp.dot(gathered, w_up, preferred_element_type=jnp.float...  73 us
    all_gather x1, waiting for transfers between devices, per_device(): gathered = lax.all_gather(normed_ffn, 'dp', axis=0, tiled=True)  53.9 us
    all_gather x1, waiting for transfers between devices, per_device(): lax.all_gather(activated, ('section', 'tensor'), axis=0, tiled=True)  50.4 us
    all_gather x1, waiting for transfers between devices, per_device(): whole = lax.all_gather(tokens, ('section', 'tensor'), axis=1, tiled=True)  40.8 us
  transfers between devices with their start and end apart: 7, of which 7 were waited for; matrix products, arithmetic and copies ran while one was open for 0% of the time, Pallas kernels for 0%

profile of v1, /device:TPU:0, one launch (start us, length us, event | category | flops | bytes accessed | tf_op | source)
XLA Modules:
  0.0 553.2 jit_solution(8000734959263812832)
XLA Ops:
  6.5 0.0 copy-start
  6.5 0.0 all-gather.4.cloned.1.call-start
  6.5 0.7 all-gather.4.cloned.1.call-update
  7.3 0.0 all-reduce.3.cloned.1.call-start
  7.3 0.9 fusion.18
  8.2 40.8 %all-gather.4.cloned.1.call-done = bf16[256,8192]{1,0:T(8,128)(2,1)} async-done(((bf16[256,512]{1,0:T(8,128)(2,1)}), bf16[256,8192]{1,0:T(8,128)(2,1)}) %all-gather.4.cloned.1.call-update) | async-done | bytes 4194320 | tf_op jit(solution)/shard_map/all_gather | solution.py:30
  49.0 3.5 convert_reduce_fusion
  52.5 0.0 copy-done.7
  52.5 0.0 copy-done.3
  52.5 0.0 copy-start.5
  52.5 1.8 fusion.3
  54.3 0.4 copy-done.5
  54.7 1.8 convolution_convert_fusion.4
  56.6 0.3 copy-done.2
  56.9 1.6 copy-done.6
  58.4 1.8 convolution_convert_fusion.5
  60.3 0.4 fusion.23
  60.7 0.3 fusion.8
  60.9 5.2 convolution_convert_fusion.6
  66.1 0.3 convolution_convert_fusion.3
  66.4 5.4 convolution_convert_fusion
  71.9 0.0 all-reduce.3.cloned.1.call-update
  71.9 0.0 all-reduce.5.cloned.1.call-start
  71.9 114.5 %all-reduce.3.cloned.1.call-done = bf16[256,8192]{1,0:T(8,128)(2,1)} async-done(((bf16[256,8192]{1,0:T(8,128)(2,1)}), bf16[256,8192]{1,0:T(8,128)(2,1)}) %all-reduce.3.cloned.1.call-update) | async-done | bytes 4194320 | tf_op jit(solution)/shard_map/psum | solution.py:22
  186.5 0.0 all-reduce.5.cloned.1.call-update
  186.5 0.2 all-gather.6.cloned.1.call-start
  186.7 0.8 dynamic-slice
  187.5 75.4 %all-reduce.5.cloned.1.call-done = bf16[256,8192]{1,0:T(8,128)(2,1)} async-done(((bf16[256,8192]{1,0:T(8,128)(2,1)}), bf16[256,8192]{1,0:T(8,128)(2,1)}) %all-reduce.5.cloned.1.call-update) | async-done | bytes 4194320 | tf_op jit(solution)/shard_map/psum | solution.py:22
  262.9 4.6 convert_reduce_fusion.1
  267.5 0.0 copy-start.4
  267.5 1.0 convert_element_type.73
  268.5 1.0 copy-done.4
  269.5 0.9 fusion.17
  270.3 0.0 all-gather.6.cloned.1.call-update
  270.4 0.0 reduce-scatter.3.cloned.1.call-start
  270.4 53.9 %all-gather.6.cloned.1.call-done = bf16[2048,512]{1,0:T(8,128)(2,1)} async-done(((bf16[256,512]{1,0:T(8,128)(2,1)}), bf16[2048,512]{1,0:T(8,128)(2,1)}) %all-gather.6.cloned.1.call-update) | async-done | bytes 2097168 | tf_op jit(solution)/shard_map/all_gather | solution.py:61
  324.3 8.3 %convolution_convert_fusion.1 = bf16[2048,2048]{1,0:T(8,128)(2,1)} fusion(bf16[2048,512]{1,0:T(8,128)(2,1)} %all-gather.6.cloned.1.call-done, bf16[512,2048]{1,0:T(8,128)(2,1)S(1)} %copy-done), kind=kOutput, calls=%fused_computation.12 | convolution fusion | flops 4299161600 | bytes 12582912 | tf_op jit(solution)/shard_map/dot_general | solution.py:63
  332.6 0.0 reduce-scatter.3.cloned.1.call-update
  332.6 0.0 all-gather.8.cloned.1.call-start
  332.7 73.0 %reduce-scatter.3.cloned.1.call-done = bf16[128,2048]{1,0:T(8,128)(2,1)} async-done(((bf16[2048,2048]{1,0:T(8,128)(2,1)}), bf16[128,2048]{1,0:T(8,128)(2,1)}) %reduce-scatter.3.cloned.1.call-update) | async-done | bytes 524304 | tf_op jit(solution)/shard_map/reduce_scatter | solution.py:62
  405.7 2.2 fusion.14
  407.9 0.0 all-gather.8.cloned.1.call-update
  408.0 0.0 reduce-scatter.5.cloned.1.call-start
  408.0 50.4 %all-gather.8.cloned.1.call-done = bf16[2048,2048]{1,0:T(8,128)(2,1)} async-done(((bf16[128,2048]{1,0:T(8,128)(2,1)}), bf16[2048,2048]{1,0:T(8,128)(2,1)}) %all-gather.8.cloned.1.call-update) | async-done | bytes 8388624 | tf_op jit(solution)/shard_map/all_gather | solution.py:70
  458.5 10.0 %convolution_convert_fusion.2 = bf16[2048,512]{1,0:T(8,128)(2,1)} fusion(bf16[2048,2048]{1,0:T(8,128)(2,1)} %all-gather.8.cloned.1.call-done, bf16[2048,512]{1,0:T(8,128)(2,1)} %param.19), kind=kOutput, calls=%fused_computation.14 | convolution fusion | flops 4296015872 | bytes 12582912 | tf_op jit(solution)/shard_map/dot_general | solution.py:69
  468.5 0.0 reduce-scatter.5.cloned.1.call-update
  468.5 76.1 %reduce-scatter.5.cloned.1.call-done = bf16[256,512]{1,0:T(8,128)(2,1)} async-done(((bf16[2048,512]{1,0:T(8,128)(2,1)}), bf16[256,512]{1,0:T(8,128)(2,1)}) %reduce-scatter.5.cloned.1.call-update) | async-done | bytes 262160 | tf_op jit(solution)/shard_map/reduce_scatter | solution.py:74
  544.5 1.8 add_convert_fusion
  (9 shorter events, 0.0 us)
Async XLA Ops:
  6.5 317.8 %copy-start = (bf16[512,2048]{1,0:T(8,128)(2,1)S(1)}, bf16[512,2048]{1,0:T(8,128)(2,1)}, u32[]{:S(2)}) copy-start(bf16[512,2048]{1,0:T(8,128)(2,1)} %param.18) | copy-start | bytes 6291460
  6.5 46.0 %copy-start.7 = (f32[8192]{0:T(1024)S(1)}, f32[8192]{0:T(1024)}, u32[]{:S(2)}) copy-start(f32[8192]{0:T(1024)} %param.12) | copy-start | bytes 98308
  6.5 42.4 %all-gather.4.cloned.1.call-start = ((), (), s32[]{:S(2)}) async-start(), calls=%async_computation.2 | async-start | bytes 4456448 | tf_op jit(solution)/shard_map/all_gather | solution.py:30
  7.3 179.2 %all-reduce.3.cloned.1.call-start = ((), (), s32[]{:S(2)}) async-start(), calls=%async_computation.3 | async-start | bytes 8388608 | tf_op jit(solution)/shard_map/psum | solution.py:22
  49.0 3.6 copy-start.3
  52.5 2.2 copy-start.5
  54.7 2.1 copy-start.2
  54.7 3.7 copy-start.6
  71.9 191.0 %all-reduce.5.cloned.1.call-start = ((), (), s32[]{:S(2)}) async-start(), calls=%async_computation.4 | async-start | bytes 8388608 | tf_op jit(solution)/shard_map/psum | solution.py:22
  186.5 137.8 %all-gather.6.cloned.1.call-start = ((), (), s32[]{:S(2)}) async-start(), calls=%async_computation.5 | async-start | bytes 2359296 | tf_op jit(solution)/shard_map/all_gather | solution.py:61
  267.5 2.0 copy-start.4
  270.4 135.3 %reduce-scatter.3.cloned.1.call-start = ((), (), s32[]{:S(2)}) async-start(), calls=%async_computation.6 | async-start | bytes 8912896 | tf_op jit(solution)/shard_map/reduce_scatter | solution.py:62
  332.6 125.8 %all-gather.8.cloned.1.call-start = ((), (), s32[]{:S(2)}) async-start(), calls=%async_computation.7 | async-start | bytes 8912896 | tf_op jit(solution)/shard_map/all_gather | solution.py:70
  408.0 136.6 %reduce-scatter.5.cloned.1.call-start = ((), (), s32[]{:S(2)}) async-start(), calls=%async_computation.8 | async-start | bytes 2359296 | tf_op jit(solution)/shard_map/reduce_scatter | solution.py:74
  458.5 87.9 %copy-start.1 = (bf16[512,2048]{1,0:T(8,128)(2,1)S(1)}, bf16[512,2048]{1,0:T(8,128)(2,1)}, u32[]{:S(2)}) copy-start(bf16[512,2048]{1,0:T(8,128)(2,1)} %param.18) | copy-start | bytes 6291460
Sparse Core Ops, SparseCore 0:
  9.0 39.8 all-gather.3
  72.0 114.3 all-reduce.2
  189.0 73.9 all-reduce.4
  270.5 53.7 all-gather.5
  332.7 72.9 reduce-scatter.2
  408.1 50.3 all-gather.7
  468.6 75.9 reduce-scatter.4
